TPU v7x, 128 devices: a whole 4x4x4 slice. The times are simulated.
128 devices in a mesh: row: 8 (over x, core), col: 16 (over z, y).
Axes of the slice: x: 4, y: 4, z: 4, core: 2. Of those that a mesh axis runs over, the one named last changes fastest.
Arguments:
- atom_feats: bfloat16 [16384, 128], P(('row', 'col')), may hold values from -6 to 6
- atom_token: int32 [16384], P(('row', 'col')), may hold values from 0 to 2047, as said below
- atom_counts: int32 [2048], P('row'), may hold values from 1 to 15, as said below
- token_cond: bfloat16 [2048, 768], P('row'), may hold values from -6 to 6
- pair: bfloat16 [2048, 2048, 128], P('row', 'col'), may hold values from -5 to 5
- token_gain: float32 [768], replicated, may hold values from 0.25 to 1.75
- pair_gain: float32 [128], replicated, may hold values from 0.25 to 1.75
- w_bias: bfloat16 [128, 16], replicated, may hold values from -4 to 4
- w_agg: bfloat16 [128, 768], replicated, may hold values from -1.5 to 1.5
- w_query: bfloat16 [768, 768], replicated, may hold values from -0.3125 to 0.3125
- w_keyval: bfloat16 [768, 1536], replicated, may hold values from -0.3125 to 0.3125
- w_out: bfloat16 [768, 768], replicated, may hold values from -0.4375 to 0.4375
- w_back: bfloat16 [768, 128], replicated, may hold values from -0.21875 to 0.21875
Outputs:
- token_out: bfloat16 [2048, 768], P('row')
- atom_out: bfloat16 [16384, 128], P(('row', 'col'))
Inputs may be any that keep to these rules, and one draw needn't show every extreme that they name: `atom_token`: atoms come in token order; the r-th block of 128 * 16 atoms belongs to tokens r * 256 to (r+1) * 256 - 1, every token has at least one atom. atom_counts[t] is the number of atoms with atom_token t; each block of 256 tokens has 2048 atoms.
All inputs are finite; a program needn't handle non-finite values.
Results may differ from a plain program's by a relative error of at most 0.023.
Values may be sent and summed in bfloat16 or wider, within the bound.
A program may use at most 128 MiB of HBM per device.

v0:
```python
import math

import jax
import jax.numpy as jnp
from jax import lax
from jax.sharding import PartitionSpec as P

D = 768
HEADS = 16


def joined(part, axis, combine):
    gathered = jax.tree.map(lambda a: lax.all_gather(a, axis), part)

    def take(source):
        return jax.tree.map(lambda a: lax.dynamic_index_in_dim(a, source, 0, False), gathered)

    return lax.fori_loop(
        1, lax.axis_size(axis), lambda source, state: combine(state, take(source)), take(0)
    )


def normalize(values):
    center = values - jnp.mean(values, axis=-1, keepdims=True)
    spread = jnp.mean(center * center, axis=-1, keepdims=True)
    return center * lax.rsqrt(spread + 1e-05)


def finish(weighted, total):
    rows_here = total.shape[0]
    return (
        (weighted.reshape(rows_here, HEADS, -1) / total[:, :, None])
        .reshape(rows_here, D)
        .astype(jnp.bfloat16)
    )


def local(
    atom_feats,
    atom_token,
    atom_counts,
    token_cond,
    pair,
    token_gain,
    pair_gain,
    w_bias,
    w_agg,
    w_query,
    w_keyval,
    w_out,
    w_back,
):
    tq_rows = atom_counts.shape[0]
    tk_rows = pair.shape[1]
    head_size = D // HEADS
    row_index = lax.axis_index("row")
    col_index = lax.axis_index("col")
    local_token = atom_token - row_index * tq_rows
    member = local_token[None, :] == jnp.arange(tq_rows, dtype=jnp.int32)[:, None]
    counts = atom_counts.astype(jnp.float32)[:, None]
    projected = jnp.dot(atom_feats, w_agg, preferred_element_type=jnp.float32)
    partial_sum = jnp.dot(member.astype(jnp.float32), projected, precision=lax.Precision.HIGHEST)
    summed = lax.psum(partial_sum.astype(jnp.bfloat16), "col").astype(jnp.float32)
    agg = summed / counts
    hidden = agg + token_cond.astype(jnp.float32)
    normed = (normalize(hidden) * token_gain).astype(jnp.bfloat16)
    query = (
        jnp.dot(normed, w_query, preferred_element_type=jnp.float32) / math.sqrt(head_size)
    ).astype(jnp.bfloat16)
    key_start = col_index * tk_rows
    everyone = lax.all_gather(normed, "row", axis=0, tiled=True)
    key_input = lax.dynamic_slice_in_dim(everyone, key_start, tk_rows, 0)
    keyval = jnp.dot(key_input, w_keyval, preferred_element_type=jnp.float32).astype(jnp.bfloat16)
    keys = keyval[:, :D].reshape(tk_rows, HEADS, head_size)
    values = keyval[:, D:].reshape(tk_rows, HEADS, head_size)
    gain_weight = (pair_gain[:, None] * w_bias.astype(jnp.float32)).astype(jnp.bfloat16)
    pair_wide = pair.astype(jnp.float32)
    pair_mean = jnp.mean(pair_wide, axis=-1)
    pair_spread = jnp.mean(jnp.square(pair_wide - pair_mean[:, :, None]), axis=-1)
    raw_bias = jnp.einsum("ijc,ch->hij", pair, gain_weight, preferred_element_type=jnp.float32)
    column_total = jnp.sum(gain_weight.astype(jnp.float32), axis=0)
    bias = (raw_bias - pair_mean[None, :, :] * column_total[:, None, None]) * lax.rsqrt(
        pair_spread + 1e-05
    )[None, :, :]
    scores = (
        jnp.einsum(
            "ihd,jhd->hij",
            query.reshape(tq_rows, HEADS, head_size),
            keys,
            preferred_element_type=jnp.float32,
        )
        + bias
    )
    local_top = jnp.transpose(jnp.max(scores, axis=-1))

    def combine(first, second):
        top = jnp.maximum(first[0], second[0])
        scale_first = jnp.exp(first[0] - top)
        scale_second = jnp.exp(second[0] - top)
        total = first[1] * scale_first + second[1] * scale_second
        rows_here = first[2].shape[0]
        weighted = (
            first[2].reshape(rows_here, HEADS, -1) * scale_first[:, :, None]
            + second[2].reshape(rows_here, HEADS, -1) * scale_second[:, :, None]
        )
        return (top, total, weighted.reshape(rows_here, -1))

    expo = jnp.exp(scores - jnp.transpose(local_top)[:, :, None])
    total = jnp.transpose(jnp.sum(expo, axis=-1))
    weighted = jnp.einsum(
        "hij,jhd->ihd", expo.astype(jnp.bfloat16), values, preferred_element_type=jnp.float32
    )
    local_weighted = weighted.reshape(tq_rows, D)
    merged = joined((local_top, total, local_weighted), "col", combine)
    attn = finish(merged[2], merged[1])
    token_out = (hidden + jnp.dot(attn, w_out, preferred_element_type=jnp.float32)).astype(
        jnp.bfloat16
    )
    back = jnp.dot(token_out, w_back, preferred_element_type=jnp.float32)
    picked = jnp.take(back, local_token, axis=0)
    atom_out = (atom_feats.astype(jnp.float32) + picked).astype(jnp.bfloat16)
    return (token_out, atom_out)


def solution(mesh):
    placed = (
        P(("row", "col"), None),
        P(("row", "col")),
        P("row"),
        P("row", None),
        P("row", "col", None),
        P(),
        P(),
        P(),
        P(),
        P(),
        P(),
        P(),
        P(),
    )
    return jax.shard_map(
        local,
        mesh=mesh,
        in_specs=placed,
        out_specs=(P("row", None), P(("row", "col"), None)),
        check_vma=False,
    )
```

profile of v0, /device:TPU:0, one launch (start us, length us, event | category | flops | bytes accessed | tf_op | source)
XLA Modules:
  0.0 354.1 jit_solution(10298502025416959507)
XLA Ops:
  11.7 87.0 %all-reduce.2.cloned.1.call-done = bf16[256,768]{1,0:T(8,128)(2,1)} async-done(((bf16[256,768]{1,0:T(8,128)(2,1)}), bf16[256,768]{1,0:T(8,128)(2,1)}) %all-reduce.2.cloned.1.call-update) | async-done | bytes 393232 | tf_op jit(solution)/shard_map/psum | solution.py:63
  98.8 1.4 fusion.19
  100.2 1.3 multiply_reduce_fusion
  101.5 2.0 multiply_convert_fusion
  103.7 5.7 %convert_reduce_fusion = f32[256,128]{1,0:T(8,128)S(1)} fusion(bf16[256,128,128]{2,1,0:T(8,128)(2,1)} %param.19), kind=kLoop, calls=%fused_computation.15 | loop fusion | flops 8355840 | bytes 8519680 | tf_op jit(solution)/shard_map/reduce_sum | solution.py:78
  110.1 10.7 %fusion.5 = f32[256,128]{1,0:T(8,128)S(1)} fusion(bf16[256,128,128]{2,1,0:T(8,128)(2,1)} %param.19, f32[256,128]{1,0:T(8,128)S(1)} %broadcast_multiply_fusion), kind=kLoop, calls=%fused_computation.17 | loop fusion | flops 16744448 | bytes 8650752 | tf_op jit(solution)/shard_map/reduce_sum | solution.py:79
  121.6 7.2 %fusion.16 = f32[16,256,128]{2,0,1:T(8,128)} fusion(bf16[256,128,128]{2,1,0:T(8,128)(2,1)} %param.19, bf16[128,16]{0,1:T(8,128)(2,1)S(1)} %copy-done.8, f32[128]{0:T(128)S(1)} %copy-done.11), kind=kOutput, calls=%fused_computation.45 | convolution fusion | flops 134223872 | bytes 10490368 | tf_op jit(solution)/shard_map/ijc,ch->hij/dot_general | solution.py:80
  128.8 3.0 copy.36
  132.4 1.7 fusion.8
  134.4 1.4 convolution_convert_fusion
  137.5 2.5 fusion.22
  139.9 1.3 copy-done.1
  144.2 23.4 %all-gather = f32[4096,16]{0,1:T(8,128)S(1)} all-gather(f32[256,16]{0,1:T(8,128)S(1)} %bitcast.79), channel_id=2, replica_groups=mesh['row'=8,'col'=16] {'col'}, dimensions={0}, use_global_device_ids=true | all-gather | bytes 278528 | tf_op jit(solution)/shard_map/all_gather | solution.py:13
  168.2 1.9 fusion.7
  170.1 22.2 %all-gather.1 = f32[4096,16]{0,1:T(8,128)S(1)} all-gather(f32[256,16]{0,1:T(8,128)S(1)} %bitcast.80), channel_id=3, replica_groups=mesh['row'=8,'col'=16] {'col'}, dimensions={0}, use_global_device_ids=true | all-gather | bytes 278528 | tf_op jit(solution)/shard_map/all_gather | solution.py:13
  194.4 39.3 %all-gather.7.cloned.1.call-done = f32[16,256,768]{2,1,0:T(8,128)} async-done(((f32[1,256,768]{2,1,0:T(8,128)}), f32[16,256,768]{2,1,0:T(8,128)}) %all-gather.7.cloned.1.call-update) | async-done | bytes 12582928 | tf_op jit(solution)/shard_map/all_gather | solution.py:13
  236.1 106.5 %while.19 = (s32[]{:T(128)}, f32[256,16]{0,1:T(8,128)}, f32[256,16]{0,1:T(8,128)}, f32[256,768]{0,1:T(8,128)}, f32[16,256,16]{1,0,2:T(8,128)}, /*index=5*/f32[16...) while((s32[]{:T(128)}, f32[256,16]{0,1:T(8,128)}, f32[256,16]{0,1:T(8,128)}, ...), condition=%wide.region_9.10_spmd, body=%wide.region_8.9_spmd.sunk | while | flops 614405 | bytes 5734551 | solution.py:18
  237.1 1.4 fusion.41
  240.8 2.4 fusion.42
  244.2 1.4 fusion.41
  247.9 2.4 fusion.42
  251.3 1.4 fusion.41
  255.0 2.4 fusion.42
  258.4 1.4 fusion.41
  262.1 2.4 fusion.42
  265.5 1.4 fusion.41
  269.2 2.4 fusion.42
  272.6 1.4 fusion.41
  276.3 2.4 fusion.42
  279.7 1.4 fusion.41
  283.4 2.4 fusion.42
  286.8 1.4 fusion.41
  290.5 2.4 fusion.42
  293.9 1.4 fusion.41
  297.6 2.4 fusion.42
  301.0 1.4 fusion.41
  304.7 2.4 fusion.42
  308.1 1.4 fusion.41
  311.8 2.4 fusion.42
  315.2 1.4 fusion.41
  318.9 2.4 fusion.42
  322.3 1.4 fusion.41
  326.0 2.4 fusion.42
  329.4 1.4 fusion.41
  333.1 2.4 fusion.42
  336.5 1.4 fusion.41
  340.2 2.4 fusion.42
  343.9 1.9 fusion.9
  (108 shorter events, 69.3 us)
Async XLA Ops:
  7.2 127.2 %copy-start = (bf16[768,1536]{1,0:T(8,128)(2,1)S(1)}, bf16[768,1536]{1,0:T(8,128)(2,1)}, u32[]{:S(2)}) copy-start(bf16[768,1536]{1,0:T(8,128)(2,1)} %param.25) | copy-start | bytes 7077892
  7.2 93.0 %copy-start.2 = (bf16[256,768]{1,0:T(8,128)(2,1)S(1)}, bf16[256,768]{1,0:T(8,128)(2,1)}, u32[]{:S(2)}) copy-start(bf16[256,768]{1,0:T(8,128)(2,1)} %param.18) | copy-start | bytes 1179652
  7.2 94.3 %copy-start.10 = (f32[768]{0:T(1024)S(1)}, f32[768]{0:T(1024)}, u32[]{:S(2)}) copy-start(f32[768]{0:T(1024)} %param.20) | copy-start | bytes 9220
  7.2 91.6 %all-reduce.2.cloned.1.call-start = ((), (), s32[]{:S(2)}) async-start(), calls=%async_computation | async-start | bytes 786432 | tf_op jit(solution)/shard_map/psum | solution.py:63
  9.7 93.9 %copy-start.13 = (s32[128]{0:T(128)}, s32[128]{0:T(128)S(1)}, u32[]{:S(2)}) copy-start(s32[128]{0:T(128)S(1)} %get-tuple-element.214) | copy-start | bytes 1540
  11.0 123.3 %all-gather.5.cloned.1.call-start = ((), (), s32[]{:S(2)}) async-start(), calls=%async_computation.1 | async-start | bytes 3538944 | tf_op jit(solution)/shard_map/all_gather | solution.py:71
  11.7 91.9 %copy-start.9 = (f32[256]{0:T(256)}, f32[256]{0:T(256)S(1)}, u32[]{:S(2)}) copy-start(f32[256]{0:T(256)S(1)} %convert_element_type.51) | copy-start | bytes 3076
  103.6 130.1 %all-gather.7.cloned.1.call-start = ((), (), s32[]{:S(2)}) async-start(), calls=%async_computation.2 | async-start | bytes 13369344 | tf_op jit(solution)/shard_map/all_gather | solution.py:13
  110.1 11.5 %copy-start.8 = (bf16[128,16]{0,1:T(8,128)(2,1)S(1)}, bf16[128,16]{0,1:T(8,128)(2,1)}, u32[]{:S(2)}) copy-start(bf16[128,16]{0,1:T(8,128)(2,1)} %param.22) | copy-start | bytes 12292
  110.1 11.5 %copy-start.11 = (f32[128]{0:T(128)S(1)}, f32[128]{0:T(128)}, u32[]{:S(2)}) copy-start(f32[128]{0:T(128)} %param.21) | copy-start | bytes 1540
  128.8 3.6 %copy-start.3 = (bf16[256,768]{1,0:T(8,128)(2,1)S(1)}, bf16[256,768]{1,0:T(8,128)(2,1)}, u32[]{:S(2)}) copy-start(bf16[256,768]{1,0:T(8,128)(2,1)} %multiply_convert_fusion) | copy-start | bytes 1179652
  137.5 3.8 %copy-start.4 = (bf16[128,768]{0,1:T(8,128)(2,1)S(1)}, bf16[128,768]{0,1:T(8,128)(2,1)}, u32[]{:S(2)}) copy-start(bf16[128,768]{0,1:T(8,128)(2,1)} %copy.38) | copy-start | bytes 589828
  139.9 1.3 copy-start.1
  343.8 2.0 copy-start.6
  343.9 3.0 copy-start.7
  343.9 3.0 copy-start.12
  345.8 1.7 copy-start.5
Sparse Core Ops, SparseCore 0:
  11.8 86.8 all-reduce.1
  103.7 26.9 all-gather.4
  143.1 90.5 all-gather.6
where the time goes:
time: 358 us; the launch traced here: 354 us
  waiting for transfers between devices  126 us (35%)
  other arithmetic  85.4 us (24%)
  local copies, waits for them, and re-layouts  64.5 us (18%)
  blocking collectives  45.6 us (13%)
  matrix products  18 us (5%)
  between operations  14 us (4%)
    psum x1, waiting for transfers between devices, local(): lax.psum(partial_sum.astype(jnp.bfloat16), 'col').astype(jnp.float32)  87 us
    dynamic_slice x47, local copies, waits for them, and re-layouts, take(): lax.dynamic_index_in_dim(a, source, 0, False)  50.9 us
    all_gather x2, blocking collectives, joined(): gathered = jax.tree.map(lambda a: lax.all_gather(a, axis), part)  45.6 us
    all_gather x1, waiting for transfers between devices, joined(): gathered = jax.tree.map(lambda a: lax.all_gather(a, axis), part)  39.3 us
    add x15, other arithmetic, combine(): first[2].reshape(rows_here, HEADS, -1) * scale_first[:, :, None]  36.3 us
    add x15, other arithmetic, combine(): total = first[1] * scale_first + second[1] * scale_second  20.4 us
    reduce_sum x1, other arithmetic, local(): jnp.mean(jnp.square(pair_wide - pair_mean[:, :, None]), axis=-1)  10.7 us
    dot_general x1, matrix products, local(): jnp.einsum('ijc,ch->hij', pair, gain_weight, preferred_element_type=jnp.f...  7.19 us
  transfers between devices with their start and end apart: 3, of which 2 were waited for; matrix products, arithmetic and copies ran while one was open for 10% of the time, Pallas kernels for 0%

commit v1 on v0

v1 whole, which is shorter than its diff:
```python
import math

import jax
import jax.numpy as jnp
from jax import lax
from jax.experimental import pallas as pl
from jax.experimental.pallas import tpu as pltpu
from jax.sharding import PartitionSpec as P

D = 768
HEADS = 16
HD = 48
CA = 128
TQ = 256
TK = 128
NCOL = 16
NROW = 8
OWN = TQ // NCOL
MSG = D + 128
CHUNK = 128
PAIR_PARTS = 8
PART_ROWS = TQ // PAIR_PARTS
FIRST_PARTS = 3
PASS_PART = 6
MESH = pl.DeviceIdType.MESH
F32 = jnp.float32
BF16 = jnp.bfloat16


def mm(a, b):
    return jnp.dot(a, b, preferred_element_type=F32)


def mm_nt(a, b):
    return lax.dot_general(a, b, (((1,), (1,)), ((), ())), preferred_element_type=F32)


def iota(shape, axis):
    return lax.broadcasted_iota(jnp.int32, shape, axis)


def split(x):
    high = x.astype(BF16)
    low = (x - high.astype(F32)).astype(BF16)
    return high, low


def rows_of(index, size):
    return pl.ds(pl.multiple_of(index * size, size), size)


def kernel(
    feats_h, tok_h, counts_h, cond_h, pair_h, tgain_h, pgain_h, wbias_h, wagg_h, wq_h, wkv_h, wo_h, wb_h,
    token_out_h, atom_out_h,
    feats, tok, counts, cond, pair, tgain, pgain, wbias, wagg, wq, wkv, wo, wb,
    gmat, colsum, bias, s1, s2, part, abuf, means, mean_own, cnt, aggv, normed, qv, kv, keymeans, keycond,
    km, vm, probs, wmsg, cbuf, expand, tokbuf, pick, atomv,
    lsem, psem, osem, asem, bsem, ksem, csem, qsem, dsem,
):
    r = lax.axis_index("row")
    c = lax.axis_index("col")
    key_col = 2 * r + lax.shift_right_logical(c, 3)
    key_slot = jnp.bitwise_and(c, 7)
    src_row = lax.shift_right_logical(c, 1)
    src_col = 8 * jnp.bitwise_and(c, 1)
    is_self = c == key_col
    other = jnp.logical_not(is_self)
    holds = r == src_row
    same_core = jnp.bitwise_and(r, 1) == jnp.bitwise_and(src_row, 1)
    sibling = jnp.bitwise_xor(r, 1)
    passes_on = jnp.logical_and(same_core, jnp.logical_not(holds))

    def col_at(offset):
        return jnp.bitwise_and(c + offset, NCOL - 1)

    next_col = col_at(1)

    def local(i, src, dst):
        return pltpu.make_async_copy(src, dst, lsem.at[i])

    loads = {
        "feats": local(0, feats_h, feats),
        "tok": local(1, tok_h, tok),
        "counts": local(2, counts_h, counts),
        "wbias": local(3, wbias_h, wbias),
        "pgain": local(4, pgain_h, pgain),
        "wagg": local(5, wagg_h, wagg),
        "cond": local(7, cond_h, cond),
        "tgain": local(8, tgain_h, tgain),
        "wq": local(9, wq_h, wq),
        "wkv": local(10, wkv_h, wkv),
        "wo": local(11, wo_h, wo),
        "wb": local(12, wb_h, wb),
    }

    def pair_load(k):
        at = pl.ds(k * PART_ROWS, PART_ROWS)
        return pltpu.make_async_copy(pair_h.at[at], pair.at[at], psem.at[k])

    for name in ("feats", "tok", "counts", "wbias", "pgain"):
        loads[name].start()

    barrier = pltpu.get_barrier_semaphore()

    def greet(row, col):
        pl.semaphore_signal(barrier, inc=1, device_id=(row, col), device_id_type=MESH)

    for k in range(1, NCOL):
        greet(r, col_at(k))
    for k in range(1, 8):
        greet(src_row, src_col + jnp.bitwise_and(c + k, 7))

    @pl.when(other)
    def _():
        greet(src_row, src_col + key_slot)

    @pl.when(jnp.logical_not(holds))
    def _():
        greet(jnp.where(same_core, src_row, sibling), c)

    for k in range(FIRST_PARTS):
        pair_load(k).start()

    loads["feats"].wait()
    loads["tok"].wait()
    here = tok[...] - r * TQ
    member = jnp.where(iota((TQ, CA), 0) == here, 1.0, 0.0).astype(BF16)
    part[...] = mm(member, feats[...]).astype(BF16)

    pl.semaphore_wait(
        barrier,
        NCOL - 1 + 8 - is_self.astype(jnp.int32) + 4 * holds.astype(jnp.int32) + passes_on.astype(jnp.int32))

    def remote(src, dst, sems, row, col):
        return pltpu.make_async_remote_copy(
            src_ref=src, dst_ref=dst, send_sem=sems.at[0], recv_sem=sems.at[1],
            device_id=(row, col), device_id_type=MESH)

    others = pl.ds(0, NCOL - 1)
    other_rows = pl.ds(0, (NCOL - 1) * OWN)

    def a_copy(peer):
        return remote(part.at[rows_of(peer, OWN)], abuf.at[c], asem, r, peer)

    a_all = remote(part.at[other_rows], abuf.at[others], asem, r, next_col)

    def each_peer(action):
        for k in (8, 9, 10, 11, 12, 13, 14, 15, 1, 2, 3, 4, 5, 6, 7):
            action(col_at(k))

    each_peer(lambda peer: a_copy(peer).start())
    for name in ("wagg", "cond", "tgain"):
        loads[name].start()
    for k in range(FIRST_PARTS, PAIR_PARTS):
        pair_load(k).start()
    for name in ("wq", "wkv", "wo", "wb"):
        loads[name].start()

    def each_target(action):
        for k in range(1, NROW):
            action(jnp.bitwise_and(r + k, NROW - 1))

        @pl.when(other)
        def _():
            action(r)

    def from_sources(buffer, sems, action):
        for count in (7, 8):
            @pl.when(is_self == (count == 7))
            def _():
                action(remote(buffer.at[pl.ds(0, count)], buffer.at[pl.ds(0, count)], sems, r, next_col))

    held_cond = cond_h.at[rows_of(jnp.bitwise_and(c, 1), TK)]

    def cond_copy(source, row):
        return remote(source, keycond, qsem, row, c)

    @pl.when(holds)
    def _():
        for k in (4, 2, 6):
            cond_copy(held_cond, jnp.bitwise_and(r + k, NROW - 1)).start()
        cond_copy(held_cond, sibling).start()

    abuf[c] = part[rows_of(c, OWN), :]

    eye = iota((CA, CA), 0) == iota((CA, CA), 1)
    eye_b = jnp.where(eye, 1.0, 0.0).astype(BF16)
    pick[...] = mm_nt(eye_b, member).astype(BF16)
    loads["wbias"].wait()
    loads["pgain"].wait()
    gain_t = (wbias[...].astype(F32) * pgain[...]).astype(BF16)
    none = jnp.zeros((HEADS, CA), BF16)
    place = iota((HEADS, CA), 0)
    ones_left = jnp.where(place == 0, 1.0, 0.0).astype(BF16)
    ones_right = jnp.where(place == 1, 1.0, 0.0).astype(BF16)
    gmat[:, 0:CA] = jnp.concatenate([gain_t, none, ones_left], axis=0)
    gmat[:, CA:2 * CA] = jnp.concatenate([none, gain_t, ones_right], axis=0)
    colsum[...] = jnp.broadcast_to(jnp.sum(gain_t.astype(F32), axis=1, keepdims=True), (HEADS, CA))
    loads["counts"].wait()
    for half in range(2):
        line = counts[:, half * CA:(half + 1) * CA].astype(F32)
        column = jnp.sum(jnp.where(eye, jnp.broadcast_to(line, (CA, CA)), 0.0), axis=1, keepdims=True)
        cnt[half * CA:(half + 1) * CA, :] = jnp.broadcast_to(column, (CA, CA))

    def bias_rows(k):
        pair_load(k).wait()

        def four(j, carry):
            first = k * PART_ROWS + 4 * j
            blocks = [jnp.transpose(pair[first + e]) for e in range(4)]
            for e in range(4):
                wide = blocks[e].astype(F32)
                s2[pl.ds(first + e, 1), :] = jnp.sum(wide * wide, axis=0, keepdims=True)
            square = jnp.concatenate(
                [jnp.concatenate(blocks[0:2], axis=1), jnp.concatenate(blocks[2:4], axis=1)], axis=0)
            sums = mm(gmat[...], square)
            for e in range(4):
                low, side = e // 2, slice((e % 2) * CA, (e % 2 + 1) * CA)
                bias[pl.ds(first + e, HEADS, stride=TQ), :] = sums[low * HEADS:(low + 1) * HEADS, side]
                s1[pl.ds(first + e, 1), :] = sums[2 * HEADS + low:2 * HEADS + low + 1, side]
            return carry

        lax.fori_loop(0, PART_ROWS // 4, four, 0, unroll=4)

    for k in range(FIRST_PARTS):
        bias_rows(k)

    a_all.wait_recv()
    own = rows_of(c, OWN)
    mean_own[...] = jnp.sum(abuf[...].astype(F32), axis=0) / cnt[own, :]
    means[own, :] = mean_own[...].astype(BF16)

    def k_copy(target):
        return remote(means.at[own], keymeans.at[key_slot], ksem, target, key_col)

    def b_copy(peer):
        return remote(means.at[own], means.at[own], bsem, r, peer)

    b_all = remote(means.at[other_rows], means.at[other_rows], bsem, r, next_col)
    each_target(lambda target: k_copy(target).start())
    each_peer(lambda peer: b_copy(peer).start())

    @pl.when(is_self)
    def _():
        keymeans[key_slot] = means[own, :]

    for k in range(FIRST_PARTS, PASS_PART):
        bias_rows(k)

    @pl.when(passes_on)
    def _():
        arrived = cond_copy(keycond, sibling)
        arrived.wait_recv()
        arrived.start()

    for k in range(PASS_PART, PAIR_PARTS):
        bias_rows(k)

    def normalize(hidden):
        center = hidden - jnp.mean(hidden, axis=-1, keepdims=True)
        spread = jnp.mean(center * center, axis=-1, keepdims=True)
        gain = jnp.concatenate([tgain[k:k + 1, :] for k in range(6)], axis=1)
        return (center * lax.rsqrt(spread + 1e-05) * gain).astype(BF16)

    for name in ("wagg", "cond", "tgain", "wq", "wkv"):
        loads[name].wait()
    @pl.when(holds)
    def _():
        keycond[...] = cond[rows_of(jnp.bitwise_and(c, 1), TK), :]

    @pl.when(jnp.logical_not(same_core))
    def _():
        cond_copy(keycond, sibling).wait_recv()

    from_sources(keymeans, ksem, lambda copy: copy.wait_recv())
    b_all.wait_recv()
    key_agg = mm(keymeans[...].reshape(TK, CA), wagg[...])
    aggv[...] = mm(means[...], wagg[...])
    key_rows = normalize(key_agg + keycond[...].astype(F32))
    for n in range(6):
        cols = slice(n * 256, (n + 1) * 256)
        kv[:, cols] = mm(key_rows, wkv[:, cols]).astype(BF16)
    for k in range(TQ // 64):
        at = slice(k * 64, (k + 1) * 64)
        normed[at, :] = normalize(aggv[at, :] + cond[at, :].astype(F32))
    for n in range(3):
        cols = slice(n * 256, (n + 1) * 256)
        qv[:, cols] = (mm(normed[...], wq[:, cols]) * (1.0 / math.sqrt(HD))).astype(BF16)

    def head_mask(first, width, head):
        lane = iota((1, width), 1) + first
        return jnp.where(jnp.logical_and(lane >= head * HD, lane < (head + 1) * HD), 1.0, 0.0).astype(BF16)

    windows = []
    for p in range(HEADS // 2):
        first = (2 * p * HD) // 128 * 128
        last = -(-((2 * p + 2) * HD) // 128) * 128
        windows.append((first, last - first))
        block = kv[:, first:last]
        for e in range(2):
            km[p, e * TK:(e + 1) * TK, 0:last - first] = block * head_mask(first, last - first, 2 * p + e)
    value_heads = []
    for n in range(3):
        heads = [h for h in range(HEADS) if h * HD < (n + 1) * 256 and (h + 1) * HD > n * 256]
        value_heads.append(heads)
        block = kv[:, D + n * 256:D + (n + 1) * 256]
        for slot, h in enumerate(heads):
            vm[n, slot * TK:(slot + 1) * TK, :] = block * head_mask(n * 256, 256, h)

    def c_copy(owner):
        return remote(wmsg.at[rows_of(owner, OWN)], cbuf.at[c], csem, r, owner)

    c_all = remote(wmsg.at[other_rows], cbuf.at[others], csem, r, next_col)
    owners = CHUNK // OWN
    chunks = TQ // CHUNK

    def attend(step):
        chunk = jnp.bitwise_and(lax.shift_right_logical(c, 3) + step, chunks - 1)
        at = rows_of(chunk, CHUNK)
        mean = s1[at, :] * (1.0 / CA)
        mean_high, mean_low = split(mean)
        mean_high = mean_high.astype(F32)
        mean_low = mean - mean_high
        var = (s2[at, :] * (1.0 / CA) - mean_high * mean_high) - mean_low * (mean_high + mean)
        rstd = lax.rsqrt(jnp.maximum(var, 0.0) + 1e-05)
        lane = iota((CHUNK, 128), 1)
        tops = jnp.zeros((CHUNK, 128), F32)
        totals = jnp.zeros((CHUNK, 128), F32)
        for p in range(HEADS // 2):
            first, width = windows[p]
            scores = mm_nt(qv[at, first:first + width], km[p, :, 0:width])
            for e in range(2):
                h = 2 * p + e
                raw = bias[pl.ds(pl.multiple_of(h * TQ + chunk * CHUNK, CHUNK), CHUNK), :]
                sc = scores[:, e * TK:(e + 1) * TK] + (raw - mean * colsum[h:h + 1, :]) * rstd
                top = jnp.max(sc, axis=-1, keepdims=True)
                expo = jnp.exp(sc - top)
                total = jnp.sum(expo, axis=-1, keepdims=True)
                probs[:, h * TK:(h + 1) * TK] = expo.astype(BF16)
                tops = jnp.where(lane == h, top, tops)
                totals = jnp.where(lane == h, total, totals)
        for n in range(3):
            heads = value_heads[n]
            wide = probs[:, heads[0] * TK:(heads[-1] + 1) * TK]
            wmsg[at, n * 256:(n + 1) * 256] = mm(wide, vm[n]).astype(BF16)
        tops_high, tops_mid = split(tops)
        tops_low = (tops - tops_high.astype(F32) - tops_mid.astype(F32)).astype(BF16)
        totals_high, totals_low = split(totals)
        stats = tops_high.astype(F32)
        for place, piece in enumerate((tops_mid, tops_low, totals_high, totals_low)):
            stats = stats + pltpu.roll(piece.astype(F32), (place + 1) * HEADS, 1)
        wmsg[at, D:MSG] = stats.astype(BF16)

        return chunk

    def far_chunk(step, carry):
        chunk = attend(step)
        for k in range(owners):
            c_copy(chunk * owners + jnp.bitwise_and(c + k, owners - 1)).start()
        return carry

    lax.fori_loop(1, chunks, far_chunk, 0)
    chunk = attend(0)
    for k in range(1, owners):
        c_copy(chunk * owners + jnp.bitwise_and(c + k, owners - 1)).start()
    cbuf[c] = wmsg[own, :]
    mean_high, mean_low = split(mean_own[...])
    hidden_own = mm(mean_high, wagg[...]) + mm(mean_low, wagg[...]) + cond[own, :].astype(F32)
    spread_row = jnp.bitwise_and(iota((256, D), 0), 127)
    spread_col = iota((256, D), 1) - spread_row * HD
    expand[...] = jnp.where(jnp.logical_and(spread_col >= 0, spread_col < HD), 1.0, 0.0).astype(BF16)
    loads["wo"].wait()
    loads["wb"].wait()
    c_all.wait_recv()

    stat = cbuf[:, :, D:MSG].reshape(TQ, 128).astype(F32)
    def piece(k):
        return pltpu.roll(stat, 128 - k * HEADS, 1)

    tops = ((stat + piece(1)) + piece(2)).reshape(NCOL, OWN, 128)
    totals = (piece(3) + piece(4)).reshape(NCOL, OWN, 128)
    best = jnp.max(tops, axis=0, keepdims=True)
    scale = jnp.exp(tops - best)
    total = jnp.sum(scale * totals, axis=0, keepdims=True)
    valid = iota((1, 1, 128), 2) < HEADS
    total = jnp.where(valid, total, 1.0)
    factor = jnp.where(valid, scale / total, 0.0).reshape(TQ, 128)
    factor = jnp.concatenate(split(factor), axis=1)
    attn_parts = []
    for n in range(3):
        cols = slice(n * 256, (n + 1) * 256)
        wide = mm(factor, expand[:, cols])
        terms = cbuf[:, :, cols].astype(F32) * wide.reshape(NCOL, OWN, 256)
        attn_parts.append(jnp.sum(terms, axis=0).astype(BF16))
    attn = jnp.concatenate(attn_parts, axis=1)
    finished = (hidden_own + mm(attn, wo[...])).astype(BF16)

    tokbuf[c] = finished
    d_all = remote(tokbuf.at[others], tokbuf.at[others], dsem, r, next_col)
    each_peer(lambda peer: remote(tokbuf.at[c], tokbuf.at[c], dsem, r, peer).start())

    a_all.wait_send()
    b_all.wait_send()

    @pl.when(holds)
    def _():
        for k in range(4):
            cond_copy(held_cond, sibling).wait_send()

    @pl.when(passes_on)
    def _():
        cond_copy(keycond, sibling).wait_send()

    from_sources(keymeans, ksem, lambda copy: copy.wait_send())
    c_all.wait_send()

    d_all.wait_recv()
    token_store = pltpu.make_async_copy(tokbuf, token_out_h, osem.at[0])
    token_store.start()
    chosen = mm(pick[...], tokbuf[...].reshape(TQ, D)).astype(BF16)
    atomv[...] = (feats[...].astype(F32) + mm(chosen, wb[...])).astype(BF16)
    atom_store = pltpu.make_async_copy(atomv, atom_out_h, osem.at[1])
    atom_store.start()
    d_all.wait_send()
    token_store.wait()
    atom_store.wait()


def hand_over(token_in, atom_in, token_out, atom_out, sems):
    copies = [
        pltpu.make_async_copy(token_in, token_out, sems.at[0]),
        pltpu.make_async_copy(atom_in, atom_out, sems.at[1]),
    ]
    for copy in copies:
        copy.start()
    for copy in copies:
        copy.wait()


def local(
    atom_feats, atom_token, atom_counts, token_cond, pair, token_gain, pair_gain, w_bias, w_agg, w_query, w_keyval,
    w_out, w_back,
):
    any_space = pl.BlockSpec(memory_space=pl.ANY)
    hbm = pl.BlockSpec(memory_space=pltpu.HBM)
    vmem = pltpu.VMEM
    dma = pltpu.SemaphoreType.DMA
    scratch = [
        vmem((CA, CA), BF16), vmem((1, CA), jnp.int32), vmem((1, TQ), jnp.int32), vmem((TQ, D), BF16),
        vmem((TQ, TK, CA), BF16), vmem((6, 128), F32), vmem((1, CA), F32), vmem((HEADS, CA), BF16),
        vmem((CA, D), BF16), vmem((D, D), BF16), vmem((D, 2 * D), BF16), vmem((D, D), BF16), vmem((D, CA), BF16),
        vmem((3 * HEADS, 2 * CA), BF16), vmem((HEADS, CA), F32), vmem((HEADS * TQ, TK), F32), vmem((TQ, TK), F32),
        vmem((TQ, TK), F32), vmem((TQ, CA), BF16), vmem((NCOL, OWN, CA), BF16), vmem((TQ, CA), BF16), vmem((OWN, CA), F32),
        vmem((TQ, CA), F32),
        vmem((TQ, D), F32), vmem((TQ, D), BF16), vmem((TQ, D), BF16), vmem((TK, 2 * D), BF16),
        vmem((8, OWN, CA), BF16), vmem((TK, D), BF16),
        vmem((HEADS // 2, 2 * TK, 256), BF16), vmem((3, 6 * TK, 256), BF16), vmem((CHUNK, HEADS * TK), BF16),
        vmem((TQ, MSG), BF16), vmem((NCOL, OWN, MSG), BF16), vmem((256, D), BF16), vmem((NCOL, OWN, D), BF16),
        vmem((CA, TQ), BF16), vmem((CA, CA), BF16),
        dma((13,)), dma((PAIR_PARTS,)), dma((2,)),
        *[dma((2,))] * 6,
    ]
    outs = pl.pallas_call(
        kernel,
        out_shape=(jax.ShapeDtypeStruct((NCOL, OWN, D), BF16), jax.ShapeDtypeStruct((CA, CA), BF16)),
        in_specs=[hbm] * 13,
        out_specs=(any_space, any_space),
        scratch_shapes=scratch,
        compiler_params=pltpu.CompilerParams(
            collective_id=0, has_side_effects=True, vmem_limit_bytes=40 * 1024 * 1024),
        name="diffusion_block",
    )(*[pltpu.with_memory_space_constraint(x, pltpu.HBM) for x in (
        atom_feats, atom_token.reshape(1, CA), atom_counts.reshape(1, TQ), token_cond, pair, token_gain.reshape(6, 128),
        pair_gain.reshape(1, CA), w_bias.T, w_agg, w_query, w_keyval, w_out, w_back,
    )])
    stored = pl.pallas_call(
        hand_over,
        out_shape=(jax.ShapeDtypeStruct((NCOL, OWN, D), BF16), jax.ShapeDtypeStruct((CA, CA), BF16)),
        in_specs=[any_space] * 2,
        out_specs=(any_space, any_space),
        scratch_shapes=[dma((2,))],
        compiler_params=pltpu.CompilerParams(vmem_limit_bytes=1024 * 1024),
        name="hand_over",
    )(*outs)
    return stored[0].reshape(TQ, D), stored[1]


def solution(mesh):
    placed = (
        P(("row", "col"), None), P(("row", "col")), P("row"), P("row", None), P("row", "col", None),
        P(), P(), P(), P(), P(), P(), P(), P(),
    )
    return jax.shard_map(
        local,
        mesh=mesh,
        in_specs=placed,
        out_specs=(P("row", None), P(("row", "col"), None)),
        check_vma=False,
    )
```

time: 358 us -> 39.5 us (0.11); the launches traced: 354 us -> 39.4 us
  waiting for transfers between devices: 126 us -> 0 us
  other arithmetic: 85.4 us -> 0 us
  local copies, waits for them, and re-layouts: 64.5 us -> 0 us
  blocking collectives: 45.6 us -> 0 us
  Pallas kernels: 0 us -> 38.7 us
  matrix products: 18 us -> 0 us
  between operations: 14 us -> 0.64 us
    psum x1 -> x0, waiting for transfers between devices: 87 us -> none  [local(): lax.psum(partial_sum.astype(jnp.bfloat16), 'col').astype(jnp.float32)]
    add x30 -> x0, other arithmetic: 56.7 us -> none  [the longest x15 36.3 us: combine(): first[2].reshape(rows_here, HEADS, -1) * scale_first[:, :, None]]
    dynamic_slice x47 -> x0, local copies, waits for them, and re-layouts: 50.9 us -> none  [take(): lax.dynamic_index_in_dim(a, source, 0, False)]
    all_gather x2 -> x0, blocking collectives: 45.6 us -> none  [joined(): gathered = jax.tree.map(lambda a: lax.all_gather(a, axis), part)]
    all_gather x2 -> x0, waiting for transfers between devices: 39.3 us -> none  [the longest x1 39.3 us: joined(): gathered = jax.tree.map(lambda a: lax.all_gather(a, axis), part)]
    pallas_call x0 -> x2, Pallas kernels: none -> 38.7 us  [the longest x1 38 us: local(): pl.pallas_call(kernel, out_shape=(jax.ShapeDtypeStruct((NCOL, OWN, D), BF...]
    reduce_sum x6 -> x0, other arithmetic: 21.6 us -> none  [the longest x1 10.7 us: local(): jnp.mean(jnp.square(pair_wide - pair_mean[:, :, None]), axis=-1)]
    dot_general x9 -> x0, matrix products: 18 us -> none  [the longest x1 7.19 us: local(): jnp.einsum('ijc,ch->hij', pair, gain_weight, preferred_element_type=jnp.f...]
  transfers between devices with their start and end apart: 3 -> 0, of which waited for: 2 -> 0; matrix products, arithmetic and copies ran while one was open for 10% -> 0% of each run, Pallas kernels for 0% -> 0%
where the time goes in v1:
time: 39.5 us; the launch traced here: 39.4 us
  Pallas kernels  38.7 us (98%)
  between operations  0.64 us (2%)
    pallas_call x1, Pallas kernels, local(): pl.pallas_call(kernel, out_shape=(jax.ShapeDtypeStruct((NCOL, OWN, D), BF...  38 us

profile of v1, /device:TPU:0, one launch (start us, length us, event | category | flops | bytes accessed | tf_op | source)
XLA Modules:
  0.0 39.4 jit_solution(15088761394930622052)
XLA Ops:
  0.6 38.0 %diffusion_block.1 = (bf16[16,16,768]{2,1,0:T(8,128)(2,1)S(1)}, bf16[128,128]{1,0:T(8,128)(2,1)S(1)}) custom-call(bf16[128,128]{1,0:T(8,128)(2,1)} %feats_h.1, s32[1,128]{1,0:T(1,128)} %bitcast.9, s32[1,256]{1,0:T(1,128)} %bitcast.8, bf16[256,768]{1,0:T(8,128)(2,1)} %cond_h.1, bf16[256,128,128]{2,1,0:T(8,128)(2,1)} %pair_h.1, f32[6,128]{1,0:T(8,128)} %bitcast.6, ...), custom_call_target="tpu_custom_call" | custom-call | tf_op jit(solution)/shard_map/diffusion_block/pallas_call | solution.py:463
  38.6 0.8 %hand_over.1 = (bf16[16,16,768]{2,1,0:T(8,128)(2,1)}, bf16[128,128]{1,0:T(8,128)(2,1)}) custom-call(bf16[16,16,768]{2,1,0:T(8,128)(2,1)S(1)} %get-tuple-element.6.token_in, bf16[128,128]{1,0:T(8,128)(2,1)S(1)} %get-tuple-element.7.atom_in), custom_call_target="tpu_custom_call" | custom-call | tf_op jit(solution)/shard_map/hand_over/pallas_call | solution.py:476

commit v2 on v1

--- a/solution.py
+++ b/solution.py
@@ -54,7 +54,7 @@
     token_out_h, atom_out_h,
     feats, tok, counts, cond, pair, tgain, pgain, wbias, wagg, wq, wkv, wo, wb,
     gmat, colsum, bias, s1, s2, part, abuf, means, mean_own, cnt, aggv, normed, qv, kv, keymeans, keycond,
-    km, vm, probs, wmsg, cbuf, expand, tokbuf, pick, atomv,
+    km, vm, probs, wmsg, cbuf, expand, tokbuf, pick, atomv, head_ones,
     lsem, psem, osem, asem, bsem, ksem, csem, qsem, dsem,
 ):
     r = lax.axis_index("row")
@@ -183,6 +183,8 @@
 
     abuf[c] = part[rows_of(c, OWN), :]
 
+    for h in range(HEADS):
+        head_ones[h * TK:(h + 1) * TK, :] = jnp.where(iota((TK, 128), 1) == h, 1.0, 0.0).astype(BF16)
     eye = iota((CA, CA), 0) == iota((CA, CA), 1)
     eye_b = jnp.where(eye, 1.0, 0.0).astype(BF16)
     pick[...] = mm_nt(eye_b, member).astype(BF16)
@@ -311,38 +313,32 @@
         return remote(wmsg.at[rows_of(owner, OWN)], cbuf.at[c], csem, r, owner)
 
     c_all = remote(wmsg.at[other_rows], cbuf.at[others], csem, r, next_col)
-    owners = CHUNK // OWN
-    chunks = TQ // CHUNK
-
-    def attend(step):
-        chunk = jnp.bitwise_and(lax.shift_right_logical(c, 3) + step, chunks - 1)
-        at = rows_of(chunk, CHUNK)
+    def attend(start, size):
+        at = pl.ds(pl.multiple_of(start, size), size)
         mean = s1[at, :] * (1.0 / CA)
         mean_high, mean_low = split(mean)
         mean_high = mean_high.astype(F32)
         mean_low = mean - mean_high
         var = (s2[at, :] * (1.0 / CA) - mean_high * mean_high) - mean_low * (mean_high + mean)
         rstd = lax.rsqrt(jnp.maximum(var, 0.0) + 1e-05)
-        lane = iota((CHUNK, 128), 1)
-        tops = jnp.zeros((CHUNK, 128), F32)
-        totals = jnp.zeros((CHUNK, 128), F32)
+        lane = iota((size, 128), 1)
+        tops = jnp.zeros((size, 128), F32)
         for p in range(HEADS // 2):
             first, width = windows[p]
             scores = mm_nt(qv[at, first:first + width], km[p, :, 0:width])
             for e in range(2):
                 h = 2 * p + e
-                raw = bias[pl.ds(pl.multiple_of(h * TQ + chunk * CHUNK, CHUNK), CHUNK), :]
+                raw = bias[pl.ds(pl.multiple_of(h * TQ + start, size), size), :]
                 sc = scores[:, e * TK:(e + 1) * TK] + (raw - mean * colsum[h:h + 1, :]) * rstd
                 top = jnp.max(sc, axis=-1, keepdims=True)
                 expo = jnp.exp(sc - top)
-                total = jnp.sum(expo, axis=-1, keepdims=True)
-                probs[:, h * TK:(h + 1) * TK] = expo.astype(BF16)
+                probs[0:size, h * TK:(h + 1) * TK] = expo.astype(BF16)
                 tops = jnp.where(lane == h, top, tops)
-                totals = jnp.where(lane == h, total, totals)
         for n in range(3):
             heads = value_heads[n]
-            wide = probs[:, heads[0] * TK:(heads[-1] + 1) * TK]
+            wide = probs[0:size, heads[0] * TK:(heads[-1] + 1) * TK]
             wmsg[at, n * 256:(n + 1) * 256] = mm(wide, vm[n]).astype(BF16)
+        totals = mm(probs[0:size, :], head_ones[...])
         tops_high, tops_mid = split(tops)
         tops_low = (tops - tops_high.astype(F32) - tops_mid.astype(F32)).astype(BF16)
         totals_high, totals_low = split(totals)
@@ -351,18 +347,19 @@
             stats = stats + pltpu.roll(piece.astype(F32), (place + 1) * HEADS, 1)
         wmsg[at, D:MSG] = stats.astype(BF16)
 
-        return chunk
-
-    def far_chunk(step, carry):
-        chunk = attend(step)
-        for k in range(owners):
-            c_copy(chunk * owners + jnp.bitwise_and(c + k, owners - 1)).start()
-        return carry
-
-    lax.fori_loop(1, chunks, far_chunk, 0)
-    chunk = attend(0)
-    for k in range(1, owners):
-        c_copy(chunk * owners + jnp.bitwise_and(c + k, owners - 1)).start()
+    plane = lax.shift_right_logical(c, 2)
+    far = 2 * jnp.bitwise_xor(lax.shift_right_logical(c, 3), 1)
+    near = jnp.bitwise_xor(plane, 1)
+    attend(64 * far, 128)
+    for k in range(4):
+        for other_plane in (2, 3):
+            c_copy(4 * jnp.bitwise_xor(plane, other_plane) + jnp.bitwise_and(c + k, 3)).start()
+    attend(64 * near, 64)
+    for k in range(4):
+        c_copy(4 * near + jnp.bitwise_and(c + k, 3)).start()
+    attend(64 * plane, 64)
+    for k in (2, 1, 3):
+        c_copy(4 * plane + jnp.bitwise_and(c + k, 3)).start()
     cbuf[c] = wmsg[own, :]
     mean_high, mean_low = split(mean_own[...])
     hidden_own = mm(mean_high, wagg[...]) + mm(mean_low, wagg[...]) + cond[own, :].astype(F32)
@@ -456,7 +453,7 @@
         vmem((8, OWN, CA), BF16), vmem((TK, D), BF16),
         vmem((HEADS // 2, 2 * TK, 256), BF16), vmem((3, 6 * TK, 256), BF16), vmem((CHUNK, HEADS * TK), BF16),
         vmem((TQ, MSG), BF16), vmem((NCOL, OWN, MSG), BF16), vmem((256, D), BF16), vmem((NCOL, OWN, D), BF16),
-        vmem((CA, TQ), BF16), vmem((CA, CA), BF16),
+        vmem((CA, TQ), BF16), vmem((CA, CA), BF16), vmem((HEADS * TK, 128), BF16),
         dma((13,)), dma((PAIR_PARTS,)), dma((2,)),
         *[dma((2,))] * 6,
     ]

time: 39.5 us -> 39.5 us (level)
  Pallas kernels: 38.7 us -> 38.3 us
where the time goes in v2:
time: 39.5 us; the launch traced here: 39 us
  Pallas kernels  38.3 us (97%)
  between operations  0.64 us (2%)
    pallas_call x1, Pallas kernels, local(): pl.pallas_call(kernel, out_shape=(jax.ShapeDtypeStruct((NCOL, OWN, D), BF...  37.6 us

profile of v2, /device:TPU:0, one launch (start us, length us, event | category | flops | bytes accessed | tf_op | source)
XLA Modules:
  0.0 39.0 jit_solution(2090479273463802712)
XLA Ops:
  0.6 37.6 %diffusion_block.1 = (bf16[16,16,768]{2,1,0:T(8,128)(2,1)S(1)}, bf16[128,128]{1,0:T(8,128)(2,1)S(1)}) custom-call(bf16[128,128]{1,0:T(8,128)(2,1)} %feats_h.1, s32[1,128]{1,0:T(1,128)} %bitcast.9, s32[1,256]{1,0:T(1,128)} %bitcast.8, bf16[256,768]{1,0:T(8,128)(2,1)} %cond_h.1, bf16[256,128,128]{2,1,0:T(8,128)(2,1)} %pair_h.1, f32[6,128]{1,0:T(8,128)} %bitcast.6, ...), custom_call_target="tpu_custom_call" | custom-call | tf_op jit(solution)/shard_map/diffusion_block/pallas_call | solution.py:460
  38.2 0.8 %hand_over.1 = (bf16[16,16,768]{2,1,0:T(8,128)(2,1)}, bf16[128,128]{1,0:T(8,128)(2,1)}) custom-call(bf16[16,16,768]{2,1,0:T(8,128)(2,1)S(1)} %get-tuple-element.6.token_in, bf16[128,128]{1,0:T(8,128)(2,1)S(1)} %get-tuple-element.7.atom_in), custom_call_target="tpu_custom_call" | custom-call | tf_op jit(solution)/shard_map/hand_over/pallas_call | solution.py:473

commit v3 on v2

--- a/solution.py
+++ b/solution.py
@@ -17,7 +17,7 @@
 NROW = 8
 OWN = TQ // NCOL
 MSG = D + 128
-CHUNK = 128
+CHUNK = 64
 PAIR_PARTS = 8
 PART_ROWS = TQ // PAIR_PARTS
 FIRST_PARTS = 3
@@ -53,7 +53,7 @@
     feats_h, tok_h, counts_h, cond_h, pair_h, tgain_h, pgain_h, wbias_h, wagg_h, wq_h, wkv_h, wo_h, wb_h,
     token_out_h, atom_out_h,
     feats, tok, counts, cond, pair, tgain, pgain, wbias, wagg, wq, wkv, wo, wb,
-    gmat, colsum, bias, s1, s2, part, abuf, means, mean_own, cnt, aggv, normed, qv, kv, keymeans, keycond,
+    gmat, colsum, bias, s1, s2, part, abuf, means, mean_own, cnt, qv, kv, keymeans, keycond,
     km, vm, probs, wmsg, cbuf, expand, tokbuf, pick, atomv, head_ones,
     lsem, psem, osem, asem, bsem, ksem, csem, qsem, dsem,
 ):
@@ -277,17 +277,15 @@
     from_sources(keymeans, ksem, lambda copy: copy.wait_recv())
     b_all.wait_recv()
     key_agg = mm(keymeans[...].reshape(TK, CA), wagg[...])
-    aggv[...] = mm(means[...], wagg[...])
     key_rows = normalize(key_agg + keycond[...].astype(F32))
     for n in range(6):
         cols = slice(n * 256, (n + 1) * 256)
         kv[:, cols] = mm(key_rows, wkv[:, cols]).astype(BF16)
-    for k in range(TQ // 64):
-        at = slice(k * 64, (k + 1) * 64)
-        normed[at, :] = normalize(aggv[at, :] + cond[at, :].astype(F32))
-    for n in range(3):
-        cols = slice(n * 256, (n + 1) * 256)
-        qv[:, cols] = (mm(normed[...], wq[:, cols]) * (1.0 / math.sqrt(HD))).astype(BF16)
+
+    def query_rows(plane):
+        at = rows_of(plane, CHUNK)
+        hidden = mm(means[at, :], wagg[...]) + cond[at, :].astype(F32)
+        qv[at, :] = (mm(normalize(hidden), wq[...]) * (1.0 / math.sqrt(HD))).astype(BF16)
 
     def head_mask(first, width, head):
         lane = iota((1, width), 1) + first
@@ -313,8 +311,9 @@
         return remote(wmsg.at[rows_of(owner, OWN)], cbuf.at[c], csem, r, owner)
 
     c_all = remote(wmsg.at[other_rows], cbuf.at[others], csem, r, next_col)
-    def attend(start, size):
-        at = pl.ds(pl.multiple_of(start, size), size)
+    def attend(plane, probs):
+        start, size = plane * CHUNK, CHUNK
+        at = rows_of(plane, CHUNK)
         mean = s1[at, :] * (1.0 / CA)
         mean_high, mean_low = split(mean)
         mean_high = mean_high.astype(F32)
@@ -332,13 +331,13 @@
                 sc = scores[:, e * TK:(e + 1) * TK] + (raw - mean * colsum[h:h + 1, :]) * rstd
                 top = jnp.max(sc, axis=-1, keepdims=True)
                 expo = jnp.exp(sc - top)
-                probs[0:size, h * TK:(h + 1) * TK] = expo.astype(BF16)
+                probs[:, h * TK:(h + 1) * TK] = expo.astype(BF16)
                 tops = jnp.where(lane == h, top, tops)
         for n in range(3):
             heads = value_heads[n]
-            wide = probs[0:size, heads[0] * TK:(heads[-1] + 1) * TK]
+            wide = probs[:, heads[0] * TK:(heads[-1] + 1) * TK]
             wmsg[at, n * 256:(n + 1) * 256] = mm(wide, vm[n]).astype(BF16)
-        totals = mm(probs[0:size, :], head_ones[...])
+        totals = mm(probs[:, :], head_ones[...])
         tops_high, tops_mid = split(tops)
         tops_low = (tops - tops_high.astype(F32) - tops_mid.astype(F32)).astype(BF16)
         totals_high, totals_low = split(totals)
@@ -348,18 +347,14 @@
         wmsg[at, D:MSG] = stats.astype(BF16)
 
     plane = lax.shift_right_logical(c, 2)
-    far = 2 * jnp.bitwise_xor(lax.shift_right_logical(c, 3), 1)
-    near = jnp.bitwise_xor(plane, 1)
-    attend(64 * far, 128)
-    for k in range(4):
-        for other_plane in (2, 3):
-            c_copy(4 * jnp.bitwise_xor(plane, other_plane) + jnp.bitwise_and(c + k, 3)).start()
-    attend(64 * near, 64)
-    for k in range(4):
-        c_copy(4 * near + jnp.bitwise_and(c + k, 3)).start()
-    attend(64 * plane, 64)
-    for k in (2, 1, 3):
-        c_copy(4 * plane + jnp.bitwise_and(c + k, 3)).start()
+    planes = [jnp.bitwise_xor(plane, k) for k in (2, 3, 1, 0)]
+    query_rows(planes[0])
+    for n, target in enumerate(planes):
+        if n < 3:
+            query_rows(planes[n + 1])
+        attend(target, probs.at[n % 2])
+        for k in (2, 1, 3, 0) if n < 3 else (2, 1, 3):
+            c_copy(4 * target + jnp.bitwise_and(c + k, 3)).start()
     cbuf[c] = wmsg[own, :]
     mean_high, mean_low = split(mean_own[...])
     hidden_own = mm(mean_high, wagg[...]) + mm(mean_low, wagg[...]) + cond[own, :].astype(F32)
@@ -449,9 +444,9 @@
         vmem((3 * HEADS, 2 * CA), BF16), vmem((HEADS, CA), F32), vmem((HEADS * TQ, TK), F32), vmem((TQ, TK), F32),
         vmem((TQ, TK), F32), vmem((TQ, CA), BF16), vmem((NCOL, OWN, CA), BF16), vmem((TQ, CA), BF16), vmem((OWN, CA), F32),
         vmem((TQ, CA), F32),
-        vmem((TQ, D), F32), vmem((TQ, D), BF16), vmem((TQ, D), BF16), vmem((TK, 2 * D), BF16),
+        vmem((TQ, D), BF16), vmem((TK, 2 * D), BF16),
         vmem((8, OWN, CA), BF16), vmem((TK, D), BF16),
-        vmem((HEADS // 2, 2 * TK, 256), BF16), vmem((3, 6 * TK, 256), BF16), vmem((CHUNK, HEADS * TK), BF16),
+        vmem((HEADS // 2, 2 * TK, 256), BF16), vmem((3, 6 * TK, 256), BF16), vmem((2, CHUNK, HEADS * TK), BF16),
         vmem((TQ, MSG), BF16), vmem((NCOL, OWN, MSG), BF16), vmem((256, D), BF16), vmem((NCOL, OWN, D), BF16),
         vmem((CA, TQ), BF16), vmem((CA, CA), BF16), vmem((HEADS * TK, 128), BF16),
         dma((13,)), dma((PAIR_PARTS,)), dma((2,)),

time: 39.5 us -> 39.9 us (1.010)
  Pallas kernels: 38.3 us -> 39 us
    pallas_call x1, Pallas kernels: 37.6 us -> 38.3 us  [local(): pl.pallas_call(kernel, out_shape=(jax.ShapeDtypeStruct((NCOL, OWN, D), BF...]
where the time goes in v3:
time: 39.9 us; the launch traced here: 39.7 us
  Pallas kernels  39 us (98%)
  between operations  0.64 us (2%)
    pallas_call x1, Pallas kernels, local(): pl.pallas_call(kernel, out_shape=(jax.ShapeDtypeStruct((NCOL, OWN, D), BF...  38.3 us

profile of v3, /device:TPU:0, one launch (start us, length us, event | category | flops | bytes accessed | tf_op | source)
XLA Modules:
  0.0 39.7 jit_solution(4550279267429785743)
XLA Ops:
  0.6 38.3 %diffusion_block.1 = (bf16[16,16,768]{2,1,0:T(8,128)(2,1)S(1)}, bf16[128,128]{1,0:T(8,128)(2,1)S(1)}) custom-call(bf16[128,128]{1,0:T(8,128)(2,1)} %feats_h.1, s32[1,128]{1,0:T(1,128)} %bitcast.9, s32[1,256]{1,0:T(1,128)} %bitcast.8, bf16[256,768]{1,0:T(8,128)(2,1)} %cond_h.1, bf16[256,128,128]{2,1,0:T(8,128)(2,1)} %pair_h.1, f32[6,128]{1,0:T(8,128)} %bitcast.6, ...), custom_call_target="tpu_custom_call" | custom-call | tf_op jit(solution)/shard_map/diffusion_block/pallas_call | solution.py:455
  38.9 0.8 %hand_over.1 = (bf16[16,16,768]{2,1,0:T(8,128)(2,1)}, bf16[128,128]{1,0:T(8,128)(2,1)}) custom-call(bf16[16,16,768]{2,1,0:T(8,128)(2,1)S(1)} %get-tuple-element.6.token_in, bf16[128,128]{1,0:T(8,128)(2,1)S(1)} %get-tuple-element.7.atom_in), custom_call_target="tpu_custom_call" | custom-call | tf_op jit(solution)/shard_map/hand_over/pallas_call | solution.py:468

commit v4 on v1

--- a/solution.py
+++ b/solution.py
@@ -20,7 +20,7 @@
 CHUNK = 128
 PAIR_PARTS = 8
 PART_ROWS = TQ // PAIR_PARTS
-FIRST_PARTS = 3
+FIRST_PARTS = 4
 PASS_PART = 6
 MESH = pl.DeviceIdType.MESH
 F32 = jnp.float32
@@ -118,7 +118,7 @@
     def _():
         greet(jnp.where(same_core, src_row, sibling), c)
 
-    for k in range(FIRST_PARTS):
+    for k in range(3):
         pair_load(k).start()
 
     loads["feats"].wait()
@@ -151,7 +151,7 @@
     each_peer(lambda peer: a_copy(peer).start())
     for name in ("wagg", "cond", "tgain"):
         loads[name].start()
-    for k in range(FIRST_PARTS, PAIR_PARTS):
+    for k in range(3, PAIR_PARTS):
         pair_load(k).start()
     for name in ("wq", "wkv", "wo", "wb"):
         loads[name].start()
@@ -220,7 +220,7 @@
                 s1[pl.ds(first + e, 1), :] = sums[2 * HEADS + low:2 * HEADS + low + 1, side]
             return carry
 
-        lax.fori_loop(0, PART_ROWS // 4, four, 0, unroll=4)
+        lax.fori_loop(0, PART_ROWS // 4, four, 0, unroll=8)
 
     for k in range(FIRST_PARTS):
         bias_rows(k)
@@ -397,7 +397,18 @@
 
     tokbuf[c] = finished
     d_all = remote(tokbuf.at[others], tokbuf.at[others], dsem, r, next_col)
-    each_peer(lambda peer: remote(tokbuf.at[c], tokbuf.at[c], dsem, r, peer).start())
+    def spread_to(peer):
+        remote(tokbuf.at[c], tokbuf.at[c], dsem, r, peer).start()
+
+    @pl.when(c != 0)
+    def _():
+        spread_to(0)
+
+    for k in (8, 7, 6, 5, 4, 3, 2, 1, 15, 14, 13, 12, 11, 10, 9):
+        @pl.when(col_at(k) != 0)
+        def _():
+            spread_to(col_at(k))
+
 
     a_all.wait_send()
     b_all.wait_send()

time: 39.5 us -> 37.5 us (0.949)
  Pallas kernels: 38.7 us -> 36.7 us
    pallas_call x1, Pallas kernels: 38 us -> 35.9 us  [local(): pl.pallas_call(kernel, out_shape=(jax.ShapeDtypeStruct((NCOL, OWN, D), BF...]
where the time goes in v4:
time: 37.5 us; the launch traced here: 37.3 us
  Pallas kernels  36.7 us (98%)
  between operations  0.64 us (2%)
    pallas_call x1, Pallas kernels, local(): pl.pallas_call(kernel, out_shape=(jax.ShapeDtypeStruct((NCOL, OWN, D), BF...  35.9 us
    pallas_call x1, Pallas kernels, local(): pl.pallas_call(hand_over, out_shape=(jax.ShapeDtypeStruct((NCOL, OWN, D),...  0.77 us

profile of v4, /device:TPU:0, one launch (start us, length us, event | category | flops | bytes accessed | tf_op | source)
XLA Modules:
  0.0 37.3 jit_solution(14706079141410386973)
XLA Ops:
  0.6 35.9 %diffusion_block.1 = (bf16[16,16,768]{2,1,0:T(8,128)(2,1)S(1)}, bf16[128,128]{1,0:T(8,128)(2,1)S(1)}) custom-call(bf16[128,128]{1,0:T(8,128)(2,1)} %feats_h.1, s32[1,128]{1,0:T(1,128)} %bitcast.9, s32[1,256]{1,0:T(1,128)} %bitcast.8, bf16[256,768]{1,0:T(8,128)(2,1)} %cond_h.1, bf16[256,128,128]{2,1,0:T(8,128)(2,1)} %pair_h.1, f32[6,128]{1,0:T(8,128)} %bitcast.6, ...), custom_call_target="tpu_custom_call" | custom-call | tf_op jit(solution)/shard_map/diffusion_block/pallas_call | solution.py:474
  36.5 0.8 %hand_over.1 = (bf16[16,16,768]{2,1,0:T(8,128)(2,1)}, bf16[128,128]{1,0:T(8,128)(2,1)}) custom-call(bf16[16,16,768]{2,1,0:T(8,128)(2,1)S(1)} %get-tuple-element.6.token_in, bf16[128,128]{1,0:T(8,128)(2,1)S(1)} %get-tuple-element.7.atom_in), custom_call_target="tpu_custom_call" | custom-call | tf_op jit(solution)/shard_map/hand_over/pallas_call | solution.py:487

commit v5 on v4

--- a/solution.py
+++ b/solution.py
@@ -74,6 +74,7 @@
         return jnp.bitwise_and(c + offset, NCOL - 1)
 
     next_col = col_at(1)
+    turn = 1 - 2 * jnp.bitwise_and(r, 1)
 
     def local(i, src, dst):
         return pltpu.make_async_copy(src, dst, lsem.at[i])
@@ -146,7 +147,7 @@
 
     def each_peer(action):
         for k in (8, 9, 10, 11, 12, 13, 14, 15, 1, 2, 3, 4, 5, 6, 7):
-            action(col_at(k))
+            action(col_at(turn * k))
 
     each_peer(lambda peer: a_copy(peer).start())
     for name in ("wagg", "cond", "tgain"):
@@ -356,13 +357,13 @@
     def far_chunk(step, carry):
         chunk = attend(step)
         for k in range(owners):
-            c_copy(chunk * owners + jnp.bitwise_and(c + k, owners - 1)).start()
+            c_copy(chunk * owners + jnp.bitwise_and(c + turn * k, owners - 1)).start()
         return carry
 
     lax.fori_loop(1, chunks, far_chunk, 0)
     chunk = attend(0)
     for k in range(1, owners):
-        c_copy(chunk * owners + jnp.bitwise_and(c + k, owners - 1)).start()
+        c_copy(chunk * owners + jnp.bitwise_and(c + turn * k, owners - 1)).start()
     cbuf[c] = wmsg[own, :]
     mean_high, mean_low = split(mean_own[...])
     hidden_own = mm(mean_high, wagg[...]) + mm(mean_low, wagg[...]) + cond[own, :].astype(F32)
@@ -405,9 +406,9 @@
         spread_to(0)
 
     for k in (8, 7, 6, 5, 4, 3, 2, 1, 15, 14, 13, 12, 11, 10, 9):
-        @pl.when(col_at(k) != 0)
+        @pl.when(col_at(turn * k) != 0)
         def _():
-            spread_to(col_at(k))
+            spread_to(col_at(turn * k))
 
 
     a_all.wait_send()

time: 37.5 us -> 37.3 us (level)
  no operation moved by 1% of the time
where the time goes in v5:
time: 37.3 us; the launch traced here: 37.2 us
  Pallas kernels  36.5 us (98%)
  between operations  0.64 us (2%)
    pallas_call x1, Pallas kernels, local(): pl.pallas_call(kernel, out_shape=(jax.ShapeDtypeStruct((NCOL, OWN, D), BF...  35.7 us
    pallas_call x1, Pallas kernels, local(): pl.pallas_call(hand_over, out_shape=(jax.ShapeDtypeStruct((NCOL, OWN, D),...  0.77 us

profile of v5, /device:TPU:0, one launch (start us, length us, event | category | flops | bytes accessed | tf_op | source)
XLA Modules:
  0.0 37.2 jit_solution(11001736369626019499)
XLA Ops:
  0.6 35.7 %diffusion_block.1 = (bf16[16,16,768]{2,1,0:T(8,128)(2,1)S(1)}, bf16[128,128]{1,0:T(8,128)(2,1)S(1)}) custom-call(bf16[128,128]{1,0:T(8,128)(2,1)} %feats_h.1, s32[1,128]{1,0:T(1,128)} %bitcast.9, s32[1,256]{1,0:T(1,128)} %bitcast.8, bf16[256,768]{1,0:T(8,128)(2,1)} %cond_h.1, bf16[256,128,128]{2,1,0:T(8,128)(2,1)} %pair_h.1, f32[6,128]{1,0:T(8,128)} %bitcast.6, ...), custom_call_target="tpu_custom_call" | custom-call | tf_op jit(solution)/shard_map/diffusion_block/pallas_call | solution.py:475
  36.4 0.8 %hand_over.1 = (bf16[16,16,768]{2,1,0:T(8,128)(2,1)}, bf16[128,128]{1,0:T(8,128)(2,1)}) custom-call(bf16[16,16,768]{2,1,0:T(8,128)(2,1)S(1)} %get-tuple-element.6.token_in, bf16[128,128]{1,0:T(8,128)(2,1)S(1)} %get-tuple-element.7.atom_in), custom_call_target="tpu_custom_call" | custom-call | tf_op jit(solution)/shard_map/hand_over/pallas_call | solution.py:488

commit v6 on v5

--- a/solution.py
+++ b/solution.py
@@ -427,22 +427,26 @@
     c_all.wait_send()
 
     d_all.wait_recv()
-    token_store = pltpu.make_async_copy(tokbuf, token_out_h, osem.at[0])
-    token_store.start()
+    token_stores = quarters(tokbuf, token_out_h, osem)
+    for copy in token_stores:
+        copy.start()
     chosen = mm(pick[...], tokbuf[...].reshape(TQ, D)).astype(BF16)
     atomv[...] = (feats[...].astype(F32) + mm(chosen, wb[...])).astype(BF16)
-    atom_store = pltpu.make_async_copy(atomv, atom_out_h, osem.at[1])
+    atom_store = pltpu.make_async_copy(atomv, atom_out_h, osem.at[4])
     atom_store.start()
     d_all.wait_send()
-    token_store.wait()
+    for copy in token_stores:
+        copy.wait()
     atom_store.wait()
 
 
+def quarters(source, target, sems):
+    parts = [pl.ds(k * (NCOL // 4), NCOL // 4) for k in range(4)]
+    return [pltpu.make_async_copy(source.at[part], target.at[part], sems.at[k]) for k, part in enumerate(parts)]
+
+
 def hand_over(token_in, atom_in, token_out, atom_out, sems):
-    copies = [
-        pltpu.make_async_copy(token_in, token_out, sems.at[0]),
-        pltpu.make_async_copy(atom_in, atom_out, sems.at[1]),
-    ]
+    copies = quarters(token_in, token_out, sems) + [pltpu.make_async_copy(atom_in, atom_out, sems.at[4])]
     for copy in copies:
         copy.start()
     for copy in copies:
@@ -469,7 +473,7 @@
         vmem((HEADS // 2, 2 * TK, 256), BF16), vmem((3, 6 * TK, 256), BF16), vmem((CHUNK, HEADS * TK), BF16),
         vmem((TQ, MSG), BF16), vmem((NCOL, OWN, MSG), BF16), vmem((256, D), BF16), vmem((NCOL, OWN, D), BF16),
         vmem((CA, TQ), BF16), vmem((CA, CA), BF16),
-        dma((13,)), dma((PAIR_PARTS,)), dma((2,)),
+        dma((13,)), dma((PAIR_PARTS,)), dma((5,)),
         *[dma((2,))] * 6,
     ]
     outs = pl.pallas_call(
@@ -490,7 +494,7 @@
         out_shape=(jax.ShapeDtypeStruct((NCOL, OWN, D), BF16), jax.ShapeDtypeStruct((CA, CA), BF16)),
         in_specs=[any_space] * 2,
         out_specs=(any_space, any_space),
-        scratch_shapes=[dma((2,))],
+        scratch_shapes=[dma((5,))],
         compiler_params=pltpu.CompilerParams(vmem_limit_bytes=1024 * 1024),
         name="hand_over",
     )(*outs)

time: 37.3 us -> 37.7 us (1.011)
  Pallas kernels: 36.5 us -> 36.9 us
    pallas_call x1, Pallas kernels: 35.7 us -> 36.1 us  [local(): pl.pallas_call(kernel, out_shape=(jax.ShapeDtypeStruct((NCOL, OWN, D), BF...]
where the time goes in v6:
time: 37.7 us; the launch traced here: 37.6 us
  Pallas kernels  36.9 us (98%)
  between operations  0.64 us (2%)
    pallas_call x1, Pallas kernels, local(): pl.pallas_call(kernel, out_shape=(jax.ShapeDtypeStruct((NCOL, OWN, D), BF...  36.1 us
    pallas_call x1, Pallas kernels, local(): pl.pallas_call(hand_over, out_shape=(jax.ShapeDtypeStruct((NCOL, OWN, D),...  0.79 us

profile of v6, /device:TPU:0, one launch (start us, length us, event | category | flops | bytes accessed | tf_op | source)
XLA Modules:
  0.0 37.6 jit_solution(15616167679832693497)
XLA Ops:
  0.6 36.1 %diffusion_block.1 = (bf16[16,16,768]{2,1,0:T(8,128)(2,1)S(1)}, bf16[128,128]{1,0:T(8,128)(2,1)S(1)}) custom-call(bf16[128,128]{1,0:T(8,128)(2,1)} %feats_h.1, s32[1,128]{1,0:T(1,128)} %bitcast.9, s32[1,256]{1,0:T(1,128)} %bitcast.8, bf16[256,768]{1,0:T(8,128)(2,1)} %cond_h.1, bf16[256,128,128]{2,1,0:T(8,128)(2,1)} %pair_h.1, f32[6,128]{1,0:T(8,128)} %bitcast.6, ...), custom_call_target="tpu_custom_call" | custom-call | tf_op jit(solution)/shard_map/diffusion_block/pallas_call | solution.py:479
  36.8 0.8 %hand_over.1 = (bf16[16,16,768]{2,1,0:T(8,128)(2,1)}, bf16[128,128]{1,0:T(8,128)(2,1)}) custom-call(bf16[16,16,768]{2,1,0:T(8,128)(2,1)S(1)} %get-tuple-element.6.token_in, bf16[128,128]{1,0:T(8,128)(2,1)S(1)} %get-tuple-element.7.atom_in), custom_call_target="tpu_custom_call" | custom-call | tf_op jit(solution)/shard_map/hand_over/pallas_call | solution.py:492

commit v7 on v5

--- a/solution.py
+++ b/solution.py
@@ -20,8 +20,8 @@
 CHUNK = 128
 PAIR_PARTS = 8
 PART_ROWS = TQ // PAIR_PARTS
-FIRST_PARTS = 4
-PASS_PART = 6
+FIRST_PARTS = 3
+PASS_PART = 5
 MESH = pl.DeviceIdType.MESH
 F32 = jnp.float32
 BF16 = jnp.bfloat16

time: 37.3 us -> 37.3 us (level)
  no operation moved by 1% of the time
where the time goes in v7:
time: 37.3 us; the launch traced here: 37.1 us
  Pallas kernels  36.5 us (98%)
  between operations  0.64 us (2%)
    pallas_call x1, Pallas kernels, local(): pl.pallas_call(kernel, out_shape=(jax.ShapeDtypeStruct((NCOL, OWN, D), BF...  35.7 us
    pallas_call x1, Pallas kernels, local(): pl.pallas_call(hand_over, out_shape=(jax.ShapeDtypeStruct((NCOL, OWN, D),...  0.77 us

profile of v7, /device:TPU:0, one launch (start us, length us, event | category | flops | bytes accessed | tf_op | source)
XLA Modules:
  0.0 37.1 jit_solution(13668004043783135966)
XLA Ops:
  0.6 35.7 %diffusion_block.1 = (bf16[16,16,768]{2,1,0:T(8,128)(2,1)S(1)}, bf16[128,128]{1,0:T(8,128)(2,1)S(1)}) custom-call(bf16[128,128]{1,0:T(8,128)(2,1)} %feats_h.1, s32[1,128]{1,0:T(1,128)} %bitcast.9, s32[1,256]{1,0:T(1,128)} %bitcast.8, bf16[256,768]{1,0:T(8,128)(2,1)} %cond_h.1, bf16[256,128,128]{2,1,0:T(8,128)(2,1)} %pair_h.1, f32[6,128]{1,0:T(8,128)} %bitcast.6, ...), custom_call_target="tpu_custom_call" | custom-call | tf_op jit(solution)/shard_map/diffusion_block/pallas_call | solution.py:475
  36.4 0.8 %hand_over.1 = (bf16[16,16,768]{2,1,0:T(8,128)(2,1)}, bf16[128,128]{1,0:T(8,128)(2,1)}) custom-call(bf16[16,16,768]{2,1,0:T(8,128)(2,1)S(1)} %get-tuple-element.6.token_in, bf16[128,128]{1,0:T(8,128)(2,1)S(1)} %get-tuple-element.7.atom_in), custom_call_target="tpu_custom_call" | custom-call | tf_op jit(solution)/shard_map/hand_over/pallas_call | solution.py:488
